TPU v7x, 32 devices: a whole 2x2x4 slice. The times are simulated.
32 devices in a mesh: node: 16 (over z, y, x), local: 2 (over core).
Axes of the slice: x: 2, y: 2, z: 4, core: 2. Of those that a mesh axis runs over, the one named last changes fastest.
Arguments:
- grad_out: bfloat16 [4096, 3584], P(('node', 'local')), may hold values from -6 to 6
- expert_ids: int32 [4096, 8], P(('node', 'local')), may hold values from 0 to 63, as said below
- gate_weights: float32 [4096, 8], P(('node', 'local')), may hold values from 0.05 to 0.35
- saved_hidden: bfloat16 [16, 64, 1024], P('node', None, 'local'), may hold values from -0.59765625 to 0.59765625
- down_weight: bfloat16 [16, 1024, 3584], P('node', 'local'), may hold values from -0.1875 to 0.1875
- second_moment: bfloat16 [16, 1024, 3584], P('node', 'local'), may hold values from 0.0019989014 to 0.25
Outputs:
- gate_weight_gradient: float32 [4096, 8], P(('node', 'local'))
- hidden_grad: bfloat16 [16, 64, 1024], P('node', None, 'local')
- new_weight: bfloat16 [16, 1024, 3584], P('node', 'local')
- new_second: bfloat16 [16, 1024, 3584], P('node', 'local')
Inputs may be any that keep to these rules, and one draw needn't show every extreme that they name: `expert_ids`: each row names 8 different experts on at most 4 nodes (node = id // 4), two on each; at most one per row is in flight (id % 4 == 0). Among the rows of one device at most 2 name the in-flight expert of any one node, and in every draw some node receives exactly 2 from every device.
All inputs are finite; a program needn't handle non-finite values.
Results may differ from a plain program's by a relative error of at most 0.0051.
Values may be sent and summed in bfloat16 or wider, within the bound.
A program may use at most 128 MiB of HBM per device.

v0:
```python
import jax
import jax.numpy as jnp
from jax import lax
from jax.sharding import PartitionSpec as P

EXPERTS_PER_HOST = 4
CAP = 2


beta_second = 0.95
learn_rate = 0.002
decay_rate = 0.1
epsilon = 1e-08
correct_second = 0.994079470779666


def gather_rows(picked_experts, gate_values, grads, node_count):
    transit_rows = picked_experts % EXPERTS_PER_HOST == 0
    row_present = jnp.any(transit_rows, 1)
    destination_node = jnp.sum(jnp.where(transit_rows, picked_experts // EXPERTS_PER_HOST, 0), 1)
    onehot = (
        (destination_node[:, None] == jnp.arange(node_count, dtype=jnp.int32)[None, :])
        & row_present[:, None]
    ).astype(jnp.int32)
    within_rank = jnp.sum(onehot * (jnp.cumsum(onehot, 0) - 1), 1)
    slot_index = destination_node * CAP + within_rank
    expert_location = (
        jnp.arange(node_count * CAP, dtype=jnp.int32)[:, None] == slot_index[None, :]
    ) & row_present[None, :]
    matched_gate = jnp.sum(jnp.where(transit_rows, gate_values, 0.0), 1).astype(jnp.bfloat16)
    departing_rows = jnp.dot(
        expert_location.astype(jnp.bfloat16), grads, preferred_element_type=jnp.float32
    ).astype(jnp.bfloat16)
    departing_gates = jnp.sum(
        jnp.where(expert_location, matched_gate.astype(jnp.float32)[None, :], 0.0), 1
    ).astype(jnp.bfloat16)
    feature_count = grads.shape[1]
    return (
        departing_rows.reshape(node_count, CAP, feature_count),
        departing_gates.reshape(node_count, CAP),
        expert_location,
        transit_rows,
    )


def on_device(grad_out, expert_ids, gate_weights, saved_hidden, down_weight, second_moment):
    node_count = lax.axis_size("node")
    members = lax.axis_size("local")
    feature_count = grad_out.shape[1]
    departing_rows, departing_gates, expert_location, transit_rows = gather_rows(
        expert_ids, gate_weights, grad_out, node_count
    )
    copies, copy_gates = (
        lax.all_gather(departing_rows[None], "local", axis=0, tiled=True),
        lax.all_gather(departing_gates[None], "local", axis=0, tiled=True),
    )
    arrived, arrived_gates = (
        lax.all_to_all(copies, "node", split_axis=1, concat_axis=1, tiled=True),
        lax.all_to_all(copy_gates, "node", split_axis=1, concat_axis=1, tiled=True),
    )
    arrived_rows = arrived.reshape(-1, feature_count)
    slot_gates = arrived_gates.reshape(-1).astype(jnp.float32)
    weight_now = down_weight[0]
    hidden_now = saved_hidden[0]
    unscaled = lax.dot_general(
        arrived_rows, weight_now, (((1,), (1,)), ((), ())), preferred_element_type=jnp.float32
    )
    hidden_out = (slot_gates[:, None] * unscaled).astype(jnp.bfloat16)
    slot_score = jnp.sum(unscaled * hidden_now.astype(jnp.float32), 1)
    scaled = (slot_gates[:, None] * arrived_rows.astype(jnp.float32)).astype(jnp.bfloat16)
    grad = lax.dot_general(
        hidden_now, scaled, (((0,), (0,)), ((), ())), preferred_element_type=jnp.float32
    )
    second_new = (
        beta_second * second_moment[0].astype(jnp.float32) + (1.0 - beta_second) * grad * grad
    )
    weight_f = weight_now.astype(jnp.float32)
    update = grad / (jnp.sqrt(second_new / correct_second) + epsilon) + decay_rate * weight_f
    weight_new = weight_f - learn_rate * update
    score_terms = slot_score.reshape(members, node_count * CAP)
    summed = lax.psum(score_terms, "local")
    own_terms = lax.dynamic_slice_in_dim(summed, lax.axis_index("local"), 1, 0)
    returned = lax.all_to_all(
        own_terms.reshape(node_count, CAP), "node", split_axis=0, concat_axis=0, tiled=True
    )
    returned_flat = returned.reshape(node_count * CAP)
    token_gradient = jnp.sum(jnp.where(expert_location, returned_flat[:, None], 0.0), 0)
    gate_weight_gradient = jnp.where(transit_rows, token_gradient[:, None], 0.0)
    return (
        gate_weight_gradient,
        hidden_out[None],
        weight_new.astype(jnp.bfloat16)[None],
        second_new.astype(jnp.bfloat16)[None],
    )


def solution(mesh):
    return jax.shard_map(
        on_device,
        mesh=mesh,
        in_specs=(
            P(("node", "local"), None),
            P(("node", "local"), None),
            P(("node", "local"), None),
            P("node", None, "local"),
            P("node", "local", None),
            P("node", "local", None),
        ),
        out_specs=(
            P(("node", "local"), None),
            P("node", None, "local"),
            P("node", "local", None),
            P("node", "local", None),
        ),
        check_vma=False,
    )
```

profile of v0, /device:TPU:0, one launch (start us, length us, event | category | flops | bytes accessed | tf_op | source)
XLA Modules:
  0.0 93.6 jit_solution(16695304097017711178)
XLA Ops:
  0.6 0.0 copy-start
  0.6 0.0 copy-start.1
  0.7 0.8 fusion.23
  1.5 0.7 fusion.20
  2.2 0.1 fusion.13
  2.3 0.2 reduce_window_sum.11
  2.4 0.2 select_reduce_fusion
  2.6 0.0 copy-done
  2.6 0.2 convolution_convert_fusion
  2.9 0.1 broadcast_in_dim_reshape.2
  3.0 2.2 %all_gather.6 = bf16[2,16,2,3584]{3,1,2,0:T(8,128)(2,1)S(1)} all-gather(bf16[1,16,2,3584]{3,1,2,0:T(8,128)(2,1)S(1)} %copy.52), channel_id=1, replica_groups=mesh['node'=16,'local'=2] {'local'}, dimensions={0}, use_global_device_ids=true | all-gather | bytes 688128 | tf_op jit(solution)/shard_map/all_gather | solution.py:54
  5.2 1.2 %copy.53 = bf16[2,16,2,3584]{3,2,0,1:T(2,128)(2,1)} copy(bf16[2,16,2,3584]{3,1,2,0:T(8,128)(2,1)S(1)} %all_gather.6) | data formatting | bytes 917504 | tf_op jit(solution)/shard_map/all_gather | solution.py:54
  6.5 0.0 copy-start.2
  6.5 8.4 %all-to-all-start = ((bf16[2,16,2,3584]{3,2,0,1:T(2,128)(2,1)}), bf16[2,16,2,3584]{3,2,0,1:T(2,128)(2,1)S(1)}, u32[]{:S(2)}, u32[]{:S(2)}) async-start(bf16[2,16,2,3584]{3,2,0,1:T(2,128)(2,1)} %copy.53), calls=%async_computation | async-start | bytes 917504 | tf_op jit(solution)/shard_map/all_to_all | solution.py:58
  14.9 14.2 %all-to-all-done = bf16[2,16,2,3584]{3,2,0,1:T(2,128)(2,1)S(1)} async-done(((bf16[2,16,2,3584]{3,2,0,1:T(2,128)(2,1)}), bf16[2,16,2,3584]{3,2,0,1:T(2,128)(2,1)S(1)}, u32[]{:S(2)}, u32[]{:S(2)}) %all-to-all-start) | async-done | bytes 458784 | tf_op jit(solution)/shard_map/all_to_all | solution.py:58
  29.0 0.3 copy.54
  29.3 0.2 reshape.62
  29.5 0.0 copy-done.1
  29.5 3.4 %multiply_reduce_fusion = (f32[64]{0:T(128)S(1)}, f32[64,512]{1,0:T(8,128)S(1)}) fusion(bf16[1,64,512]{2,1,0:T(8,128)(2,1)S(1)} %copy-done.1, bf16[64,3584]{1,0:T(8,128)(2,1)S(1)} %reshape.62, bf16[1,512,3584]{2,1,0:T(8,128)(2,1)} %param.10), kind=kOutput, calls=%fused_computation.16 | convolution fusion | flops 234979264 | bytes 4325632 | tf_op jit(solution)/shard_map/dot_general | solution.py:65
  32.9 0.1 reshape.63
  33.0 2.5 %psum.7 = f32[2,32]{1,0:T(2,128)S(1)} all-reduce(f32[2,32]{1,0:T(2,128)S(1)} %reshape.63), channel_id=1, replica_groups=mesh['node'=16,'local'=2] {'local'}, use_global_device_ids=true, to_apply=%region_5.6 | all-reduce | flops 64 | bytes 512 | tf_op jit(solution)/shard_map/psum | solution.py:81
  35.5 0.7 all_to_all.13
  36.2 3.8 %all-to-all-start.1 = ((f32[16,1,2]{2,1,0:T(1,128)}), f32[16,1,2]{2,1,0:T(1,128)S(1)}, u32[]{:S(2)}, u32[]{:S(2)}) async-start(f32[16,1,2]{2,1,0:T(1,128)} %bitcast.2), calls=%async_computation.1 | async-start | bytes 16384 | tf_op jit(solution)/shard_map/all_to_all | solution.py:83
  39.9 0.0 copy-done.2
  40.0 5.9 %copy.55 = bf16[1,512,3584]{1,2,0:T(8,128)(2,1)} copy(bf16[1,512,3584]{2,1,0:T(8,128)(2,1)} %param.10) | data formatting | bytes 7340032 | tf_op args[4]
  45.9 1.2 %all-to-all-done.1 = f32[16,1,2]{2,1,0:T(1,128)S(1)} async-done(((f32[16,1,2]{2,1,0:T(1,128)}), f32[16,1,2]{2,1,0:T(1,128)S(1)}, u32[]{:S(2)}, u32[]{:S(2)}) %all-to-all-start.1) | async-done | bytes 160 | tf_op jit(solution)/shard_map/all_to_all | solution.py:83
  47.1 0.5 broadcast.47
  47.6 0.7 reduce.7
  48.3 0.1 broadcast_in_dim.59
  48.4 0.1 select_reduce_fusion.1
  48.5 0.1 convert_element_type.82
  48.6 0.1 copy.57
  48.7 5.9 %copy.63 = bf16[1,512,3584]{1,2,0:T(8,128)(2,1)} copy(bf16[1,512,3584]{2,1,0:T(8,128)(2,1)} %param.11) | data formatting | bytes 7340032 | tf_op args[5]
  54.6 1.8 %all_gather.7 = bf16[2,16,2]{1,2,0:T(2,128)(2,1)S(1)} all-gather(bf16[1,16,2]{1,2,0:T(2,128)(2,1)S(1)} %copy.57), channel_id=1, replica_groups=mesh['node'=16,'local'=2] {'local'}, dimensions={0}, use_global_device_ids=true | all-gather | bytes 192 | tf_op jit(solution)/shard_map/all_gather | solution.py:55
  56.4 0.7 copy.58
  57.1 5.7 %all-to-all-start.2 = ((bf16[2,16,2]{2,0,1:T(2,128)(2,1)}), bf16[2,16,2]{2,0,1:T(2,128)(2,1)S(1)}, u32[]{:S(2)}, u32[]{:S(2)}) async-start(bf16[2,16,2]{2,0,1:T(2,128)(2,1)} %copy.58), calls=%async_computation.2 | async-start | bytes 16384 | tf_op jit(solution)/shard_map/all_to_all | solution.py:59
  62.8 0.6 broadcast_select_fusion
  63.4 6.6 %all-to-all-done.2 = bf16[2,16,2]{2,0,1:T(2,128)(2,1)S(1)} async-done(((bf16[2,16,2]{2,0,1:T(2,128)(2,1)}), bf16[2,16,2]{2,0,1:T(2,128)(2,1)S(1)}, u32[]{:S(2)}, u32[]{:S(2)}) %all-to-all-start.2) | async-done | bytes 160 | tf_op jit(solution)/shard_map/all_to_all | solution.py:59
  70.0 0.1 copy.60
  70.1 0.1 multiply_convert_fusion
  70.2 0.5 copy.62
  70.7 0.2 convert_element_type.90
  70.9 0.1 reshape.64
  71.0 10.1 %fusion.5 = (bf16[1,512,3584]{1,2,0:T(8,128)(2,1)}, bf16[1,512,3584]{1,2,0:T(8,128)(2,1)}) fusion(bf16[1,512,3584]{1,2,0:T(8,128)(2,1)} %copy.63, bf16[1,512,3584]{1,2,0:T(8,128)(2,1)} %copy.55, bf16[64,3584]{1,0:T(8,128)(2,1)S(1)} %convert_element_type.90, bf16[1,64,512]{2,1,0:T(8,128)(2,1)S(1)} %copy-done.1), kind=kOutput, calls=%fused_computation.10 | convolution fusion | flops 262406144 | bytes 15204352 | tf_op jit(solution)/shard_map/dot_general | solution.py:71
  81.1 5.9 %copy.65 = bf16[1,512,3584]{2,1,0:T(8,128)(2,1)} copy(bf16[1,512,3584]{1,2,0:T(8,128)(2,1)} %get-tuple-element.32) | data formatting | bytes 7340032
  87.0 5.9 %copy.64 = bf16[1,512,3584]{2,1,0:T(8,128)(2,1)} copy(bf16[1,512,3584]{1,2,0:T(8,128)(2,1)} %get-tuple-element.33) | data formatting | bytes 7340032
  92.9 0.7 fusion.9
  (6 shorter events, 0.1 us)
Async XLA Ops:
  0.6 2.0 %copy-start = (bf16[128,3584]{1,0:T(8,128)(2,1)S(1)}, bf16[128,3584]{1,0:T(8,128)(2,1)}, u32[]{:S(2)}) copy-start(bf16[128,3584]{1,0:T(8,128)(2,1)} %param.6) | copy-start | bytes 2752516
  0.6 28.9 %copy-start.1 = (bf16[1,64,512]{2,1,0:T(8,128)(2,1)S(1)}, bf16[1,64,512]{2,1,0:T(8,128)(2,1)}, u32[]{:S(2)}) copy-start(bf16[1,64,512]{2,1,0:T(8,128)(2,1)} %param.9) | copy-start | bytes 196612
  6.5 33.5 %copy-start.2 = (f32[128,8]{0,1:T(8,128)S(1)}, f32[128,8]{0,1:T(8,128)}, u32[]{:S(2)}) copy-start(f32[128,8]{0,1:T(8,128)} %param.8) | copy-start | bytes 12292
  6.5 22.5 %all-to-all-start = ((bf16[2,16,2,3584]{3,2,0,1:T(2,128)(2,1)}), bf16[2,16,2,3584]{3,2,0,1:T(2,128)(2,1)S(1)}, u32[]{:S(2)}, u32[]{:S(2)}) async-start(bf16[2,16,2,3584]{3,2,0,1:T(2,128)(2,1)} %copy.53), calls=%async_computation | async-start | bytes 917504 | tf_op jit(solution)/shard_map/all_to_all | solution.py:58
  36.2 11.0 %all-to-all-start.1 = ((f32[16,1,2]{2,1,0:T(1,128)}), f32[16,1,2]{2,1,0:T(1,128)S(1)}, u32[]{:S(2)}, u32[]{:S(2)}) async-start(f32[16,1,2]{2,1,0:T(1,128)} %bitcast.2), calls=%async_computation.1 | async-start | bytes 16384 | tf_op jit(solution)/shard_map/all_to_all | solution.py:83
  57.1 12.9 %all-to-all-start.2 = ((bf16[2,16,2]{2,0,1:T(2,128)(2,1)}), bf16[2,16,2]{2,0,1:T(2,128)(2,1)S(1)}, u32[]{:S(2)}, u32[]{:S(2)}) async-start(bf16[2,16,2]{2,0,1:T(2,128)(2,1)} %copy.58), calls=%async_computation.2 | async-start | bytes 16384 | tf_op jit(solution)/shard_map/all_to_all | solution.py:59
where the time goes:
time: 94.5 us; the launch traced here: 93.6 us
  local copies, waits for them, and re-layouts  28.7 us (30%)
  waiting for transfers between devices  22 us (23%)
  starting transfers between devices  17.8 us (19%)
  matrix products  13.7 us (14%)
  blocking collectives  6.43 us (7%)
  other arithmetic  4.22 us (4%)
    unnamed x10, local copies, waits for them, and re-layouts  23.7 us
    all_to_all x1, waiting for transfers between devices, on_device(): lax.all_to_all(copies, 'node', split_axis=1, concat_axis=1, tiled=True)  14.2 us
    dot_general x1, matrix products, on_device(): lax.dot_general(hidden_now, scaled, (((0,), (0,)), ((), ())), preferred_e...  10.1 us
    all_to_all x1, starting transfers between devices, on_device(): lax.all_to_all(copies, 'node', split_axis=1, concat_axis=1, tiled=True)  8.37 us
    all_to_all x1, waiting for transfers between devices, on_device(): lax.all_to_all(copy_gates, 'node', split_axis=1, concat_axis=1, tiled=True)  6.6 us
    all_to_all x1, starting transfers between devices, on_device(): lax.all_to_all(copy_gates, 'node', split_axis=1, concat_axis=1, tiled=True)  5.67 us
    all_to_all x1, starting transfers between devices, on_device(): lax.all_to_all(own_terms.reshape(node_count, CAP), 'node', split_axis=0,...  3.76 us
    dot_general x1, matrix products, on_device(): lax.dot_general(arrived_rows, weight_now, (((1,), (1,)), ((), ())), prefe...  3.37 us
  transfers between devices with their start and end apart: 3, of which 3 were waited for; matrix products, arithmetic and copies ran while one was open for 7% of the time, Pallas kernels for 0%

commit v1 on v0

v1 whole, which is shorter than its diff:
```python
import functools

import jax
import jax.numpy as jnp
from jax import lax
from jax.experimental import pallas as pl
from jax.experimental.pallas import tpu as pltpu
from jax.sharding import PartitionSpec as P

MESH = pl.DeviceIdType.MESH
EXPERTS_PER_HOST = 4
CAP = 2
WIDTH = 256
SLAB = 16
BLOCKS = SLAB // CAP
LANES = 128

beta_second = 0.95
learn_rate = 0.002
decay_rate = 0.1
epsilon = 1e-08
correct_second = 0.994079470779666

f32 = jnp.float32
bf16 = jnp.bfloat16


def dot(a, b, dims=((1,), (0,))):
    return lax.dot_general(a, b, (dims, ((), ())), preferred_element_type=f32)


def iota(shape, axis):
    return lax.broadcasted_iota(jnp.int32, shape, axis)


def kernel(
    nodes, members, plan,
    ids_ref, gates_ref, grad_hbm, hidden_hbm, weight_hbm, second_hbm,
    score_out, hidden_out, weight_out, second_out,
    grads, hidden, weight, second, hidden_t, send, recv, picks, x, scaled, gate,
    unscaled, score_send, score_recv,
    load_sem, send_sem, recv_sem, pass_sem, score_send_sem, score_recv_sem,
):
    n, l = lax.axis_index("node"), lax.axis_index("local")
    devices = nodes * members
    me = l * nodes + n
    tokens = grads.shape[0]
    slots, units = hidden.shape
    group = min(32, devices)

    loads = [
        pltpu.make_async_copy(source, target, load_sem.at[i])
        for i, (source, target) in enumerate(
            ((grad_hbm, grads), (hidden_hbm, hidden), (weight_hbm, weight), (second_hbm, second))
        )
    ]
    for load in loads:
        load.start()

    barrier = pltpu.get_barrier_semaphore()

    def greet(k, carry):
        other = lax.rem(me + k, devices)
        pl.semaphore_signal(
            barrier, inc=1, device_id=(lax.rem(other, nodes), other // nodes), device_id_type=MESH
        )
        return carry

    lax.fori_loop(1, devices, greet, 0)

    ids = ids_ref[...]
    hit = ids % EXPERTS_PER_HOST == 0
    hit_one = jnp.where(hit, 1, 0)
    present = jnp.max(hit_one, 0, keepdims=True)
    dest = jnp.sum(jnp.where(hit, ids // EXPERTS_PER_HOST, 0), 0, keepdims=True)
    dest = jnp.where(present > 0, dest, -1)
    onehot = jnp.where(iota((nodes, tokens), 0) == dest, 1.0, 0.0).astype(f32)
    before = jnp.where(iota((tokens, tokens), 0) < iota((tokens, tokens), 1), 1.0, 0.0)
    earlier = dot(onehot.astype(bf16), before.astype(bf16))
    rank = jnp.sum(onehot * earlier, 0, keepdims=True).astype(jnp.int32)
    key = jnp.where(present > 0, dest * SLAB + rank, -SLAB * CAP)
    matched = jnp.sum(jnp.where(hit, gates_ref[...], 0.0), 0, keepdims=True)
    matched = matched.astype(bf16).astype(f32)

    loads[0].wait()
    place = iota((nodes * SLAB, tokens), 0)

    def pack(q):
        total = jnp.zeros((nodes * SLAB, WIDTH), f32)
        for c, block in enumerate(plan[q]):
            mask = place == key + CAP * c
            if block is None:
                total += dot(
                    jnp.where(mask, matched, 0.0).astype(bf16), jnp.ones((tokens, WIDTH), bf16)
                )
            else:
                total += dot(
                    jnp.where(mask, 1.0, 0.0).astype(bf16),
                    grads[:, block * WIDTH:(block + 1) * WIDTH],
                )
        send[q] = total.astype(bf16).reshape(nodes, SLAB, WIDTH)

    def push(q):
        def one(k, carry):
            other = lax.rem(n + k, nodes)
            pltpu.make_async_remote_copy(
                src_ref=send.at[q, other], dst_ref=recv.at[q, me],
                send_sem=send_sem.at[q], recv_sem=recv_sem.at[q, me],
                device_id=(other, l), device_id_type=MESH,
            ).start()
            return carry

        lax.fori_loop(1, nodes, one, 0)
        recv[q, me] = send[q, n]

    def hand_on(q, source):
        for k in range(1, members):
            pltpu.make_async_remote_copy(
                src_ref=recv.at[q, source], dst_ref=recv.at[q, source],
                send_sem=pass_sem.at[q], recv_sem=recv_sem.at[q, source],
                device_id=(n, lax.rem(l + k, members)), device_id_type=MESH,
            ).start()

    def arrival(q, source):
        return pltpu.make_async_copy(
            recv.at[q, source], recv.at[q, source], recv_sem.at[q, source]
        )

    def gather(q):
        def direct(k, carry):
            source = l * nodes + lax.rem(n + nodes - k, nodes)
            arrival(q, source).wait()
            hand_on(q, source)
            return carry

        lax.fori_loop(1, nodes, direct, 0)

        def passed(k, carry):
            source = lax.rem(l * nodes + nodes + k, devices)
            arrival(q, source).wait()
            return carry

        lax.fori_loop(0, devices - nodes, passed, 0)

    def unpack(q):
        for g in range(devices // group):
            landed = recv[q, g * group:(g + 1) * group].reshape(group * SLAB, WIDTH)
            chosen = dot(picks[...], landed)
            rows = group * CAP
            here = slice(g * rows, (g + 1) * rows)
            for c, block in enumerate(plan[q]):
                if block is None:
                    gate[here, :] = chosen[c * rows:(c + 1) * rows]
            for c, block in enumerate(plan[q]):
                if block is not None:
                    part = chosen[c * rows:(c + 1) * rows]
                    columns = slice(block * WIDTH, (block + 1) * WIDTH)
                    x[here, columns] = part.astype(bf16)
                    scaled[here, columns] = (gate[here, :] * part).astype(bf16)

    def span(q):
        blocks = [b for b in plan[q] if b is not None]
        return blocks[0] * WIDTH, (blocks[-1] + 1) * WIDTH

    def multiply(q):
        first, last = span(q)
        part = dot(x[:, first:last], weight[:, first:last], ((1,), (1,)))
        unscaled[...] = part if q == 0 else unscaled[...] + part

    tall = min(256, units)

    def update(q):
        first, last = span(q)

        def tile(i, carry):
            rows = pl.ds(pl.multiple_of(lax.rem(i, units // tall) * tall, tall), tall)
            columns = pl.ds(pl.multiple_of(first + (i // (units // tall)) * WIDTH, WIDTH), WIDTH)
            grad = dot(hidden_t[rows, :], scaled[:, columns])
            second_new = (
                beta_second * second[rows, columns].astype(f32)
                + ((1.0 - beta_second) * grad) * grad
            )
            y = second_new * (1.0 / correct_second)
            root = y * lax.rsqrt(y)
            step = (learn_rate * grad) * pl.reciprocal(root + epsilon, approx=True)
            weight_new = weight[rows, columns].astype(f32) * (1.0 - learn_rate * decay_rate) - step
            second_out[rows, columns] = second_new.astype(bf16)
            weight_out[rows, columns] = weight_new.astype(bf16)
            return carry

        lax.fori_loop(0, (units // tall) * ((last - first) // WIDTH), tile, 0)

    pack(0)
    pl.semaphore_wait(barrier, devices - 1)
    push(0)
    for q in range(1, len(plan)):
        pack(q)
        push(q)
    for q in range(len(plan)):
        hand_on(q, me)

    picked_row, picked_col = iota((group * CAP, group * SLAB), 0), iota((group * CAP, group * SLAB), 1)
    wanted = (picked_row // CAP) * SLAB + picked_row % CAP
    for c in range(BLOCKS):
        picks[c * group * CAP:(c + 1) * group * CAP, :] = jnp.where(
            picked_col == wanted + CAP * c, 1.0, 0.0
        ).astype(bf16)
    loads[1].wait()
    hidden_t[...] = hidden[...].astype(f32).T.astype(bf16)
    loads[2].wait()
    loads[3].wait()

    for q in range(len(plan)):
        gather(q)
        unpack(q)
        multiply(q)
        if q < len(plan) - 1:
            update(q)

    raw = unscaled[...]
    for j in range(0, units, LANES):
        hidden_out[:, j:j + LANES] = (gate[:, :LANES] * raw[:, j:j + LANES]).astype(bf16)
    terms = raw * hidden[...].astype(f32)
    folded = terms[:, :LANES]
    for j in range(LANES, units, LANES):
        folded += terms[:, j:j + LANES]
    for s in range(0, slots, LANES):
        part = folded[s:s + LANES]
        if part.shape[0] < LANES:
            part = jnp.concatenate([part, jnp.zeros((LANES - part.shape[0], LANES), f32)], 0)
        score_send[s // LANES] = jnp.sum(part.T, 0, keepdims=True)

    def answer(k, carry):
        other = lax.rem(me + k, devices)
        pltpu.make_async_remote_copy(
            src_ref=score_send.at[(CAP * other) // LANES], dst_ref=score_recv.at[me],
            send_sem=score_send_sem, recv_sem=score_recv_sem,
            device_id=(lax.rem(other, nodes), other // nodes), device_id_type=MESH,
        ).start()
        return carry

    lax.fori_loop(1, devices, answer, 0)
    score_recv[me] = score_send[(CAP * me) // LANES]

    update(len(plan) - 1)

    others = score_recv.at[pl.ds(0, devices - 1)]
    pltpu.make_async_copy(others, others, score_recv_sem).wait()
    sums = score_recv[0:nodes].reshape(nodes, LANES)
    for k in range(1, members):
        sums += score_recv[k * nodes:(k + 1) * nodes].reshape(nodes, LANES)
    lane = iota((nodes, LANES), 1) - lax.rem(CAP * me, LANES)
    token_score = jnp.zeros((1, tokens), f32)
    for r in range(CAP):
        column = jnp.sum(jnp.where(lane == r, sums, 0.0), 1, keepdims=True)
        column = jnp.sum(jnp.where(onehot > 0, column, 0.0), 0, keepdims=True)
        token_score += jnp.where(rank == r, column, 0.0)
    score_out[...] = jnp.where(hit, token_score, 0.0)

    pltpu.make_async_copy(others, others, score_send_sem).wait()
    for q in range(len(plan)):
        sent = send.at[q, pl.ds(0, nodes - 1)]
        pltpu.make_async_copy(sent, sent, send_sem.at[q]).wait()
        if members > 1:
            for _ in range(1):
                given = recv.at[q, pl.ds(0, nodes * (members - 1))]
                pltpu.make_async_copy(given, given, pass_sem.at[q]).wait()


def on_device(nodes, members, grad_out, expert_ids, gate_weights, saved_hidden, down_weight, second_moment):
    tokens, features = grad_out.shape
    _, slots, units = saved_hidden.shape
    devices = nodes * members
    group = min(32, devices)
    blocks = [None] + list(range(features // WIDTH))
    plan = [blocks[i:i + BLOCKS] for i in range(0, len(blocks), BLOCKS)]
    chunks = len(plan)
    small = pl.BlockSpec(memory_space=pltpu.VMEM)
    large = pl.BlockSpec(memory_space=pl.ANY)
    scores, hidden_grad, new_weight, new_second = pl.pallas_call(
        functools.partial(kernel, nodes, members, plan),
        out_shape=(
            pltpu.VMEM((expert_ids.shape[1], tokens), f32),
            pltpu.VMEM((slots, units), bf16),
            pltpu.VMEM((units, features), bf16),
            pltpu.VMEM((units, features), bf16),
        ),
        in_specs=[small, small, large, large, large, large],
        out_specs=(small, small, small, small),
        scratch_shapes=[
            pltpu.VMEM((tokens, features), bf16),
            pltpu.VMEM((slots, units), bf16),
            pltpu.VMEM((units, features), bf16),
            pltpu.VMEM((units, features), bf16),
            pltpu.VMEM((units, slots), bf16),
            pltpu.VMEM((chunks, nodes, SLAB, WIDTH), bf16),
            pltpu.VMEM((chunks, devices, SLAB, WIDTH), bf16),
            pltpu.VMEM((BLOCKS * group * CAP, group * SLAB), bf16),
            pltpu.VMEM((slots, features), bf16),
            pltpu.VMEM((slots, features), bf16),
            pltpu.VMEM((slots, WIDTH), f32),
            pltpu.VMEM((slots, units), f32),
            pltpu.VMEM((-(-slots // LANES), 1, LANES), f32),
            pltpu.VMEM((devices, 1, LANES), f32),
            pltpu.SemaphoreType.DMA((4,)),
            pltpu.SemaphoreType.DMA((chunks,)),
            pltpu.SemaphoreType.DMA((chunks, devices)),
            pltpu.SemaphoreType.DMA((chunks,)),
            pltpu.SemaphoreType.DMA,
            pltpu.SemaphoreType.DMA,
        ],
        compiler_params=pltpu.CompilerParams(
            collective_id=0, has_side_effects=True, vmem_limit_bytes=48 * 1024 * 1024
        ),
        cost_estimate=pl.CostEstimate(
            flops=4 * slots * units * features, bytes_accessed=8 * units * features, transcendentals=0
        ),
    )(expert_ids.T, gate_weights.T, grad_out, saved_hidden[0], down_weight[0], second_moment[0])
    return scores.T, hidden_grad[None], new_weight[None], new_second[None]


def solution(mesh):
    return jax.shard_map(
        functools.partial(on_device, mesh.shape["node"], mesh.shape["local"]),
        mesh=mesh,
        in_specs=(
            P(("node", "local"), None),
            P(("node", "local"), None),
            P(("node", "local"), None),
            P("node", None, "local"),
            P("node", "local", None),
            P("node", "local", None),
        ),
        out_specs=(
            P(("node", "local"), None),
            P("node", None, "local"),
            P("node", "local", None),
            P("node", "local", None),
        ),
        check_vma=False,
    )
```

time: 94.5 us -> 33.4 us (0.35)
  Pallas kernels: 0 us -> 27.7 us
  local copies, waits for them, and re-layouts: 28.7 us -> 4.9 us
  waiting for transfers between devices: 22 us -> 0 us
  starting transfers between devices: 17.8 us -> 0 us
  matrix products: 13.7 us -> 0 us
  blocking collectives: 6.43 us -> 0 us
  other arithmetic: 4.22 us -> 0 us
    pallas_call x0 -> x1, Pallas kernels: none -> 27.7 us  [on_device(): pl.pallas_call(functools.partial(kernel, nodes, members, plan), out_shape...]
    all_to_all x3 -> x0, waiting for transfers between devices: 22 us -> none  [the longest x1 14.2 us: on_device(): lax.all_to_all(copies, 'node', split_axis=1, concat_axis=1, tiled=True)]
    unnamed x10 -> x4, local copies, waits for them, and re-layouts: 23.7 us -> 4.9 us
    all_to_all x3 -> x0, starting transfers between devices: 17.8 us -> none  [the longest x1 8.37 us: on_device(): lax.all_to_all(copies, 'node', split_axis=1, concat_axis=1, tiled=True)]
    dot_general x3 -> x0, matrix products: 13.7 us -> none  [the longest x1 10.1 us: on_device(): lax.dot_general(hidden_now, scaled, (((0,), (0,)), ((), ())), preferred_e...]
    all_gather x2 -> x0, blocking collectives: 3.97 us -> none  [the longest x1 2.21 us: on_device(): lax.all_gather(departing_rows[None], 'local', axis=0, tiled=True)]
    psum x1 -> x0, blocking collectives: 2.46 us -> none  [on_device(): summed = lax.psum(score_terms, 'local')]
    all_gather x2 -> x0, local copies, waits for them, and re-layouts: 1.94 us -> none  [the longest x1 1.24 us: on_device(): lax.all_gather(departing_rows[None], 'local', axis=0, tiled=True)]
  transfers between devices with their start and end apart: 3 -> 0, of which waited for: 3 -> 0; matrix products, arithmetic and copies ran while one was open for 7% -> 0% of each run, Pallas kernels for 0% -> 0%
where the time goes in v1:
time: 33.4 us; the launch traced here: 33.2 us
  Pallas kernels  27.7 us (83%)
  local copies, waits for them, and re-layouts  4.9 us (15%)
  between operations  0.64 us (2%)
    pallas_call x1, Pallas kernels, on_device(): pl.pallas_call(functools.partial(kernel, nodes, members, plan), out_shape...  27.7 us
    unnamed x4, local copies, waits for them, and re-layouts  4.9 us

profile of v1, /device:TPU:0, one launch (start us, length us, event | category | flops | bytes accessed | tf_op | source)
XLA Modules:
  0.0 33.2 jit_solution(7378387926247646089)
XLA Ops:
  0.6 27.7 %shard_map.93 = (f32[8,128]{1,0:T(8,128)S(1)}, bf16[64,512]{1,0:T(8,128)(2,1)S(1)}, bf16[512,3584]{1,0:T(8,128)(2,1)S(1)}, bf16[512,3584]{1,0:T(8,128)(2,1)S(1)}) custom-call(s32[8,128]{1,0:T(8,128)} %bitcast.16, f32[8,128]{1,0:T(8,128)} %bitcast.17, bf16[128,3584]{1,0:T(8,128)(2,1)} %grad_hbm.1, bf16[64,512]{1,0:T(8,128)(2,1)} %bitcast.15, ...), custom_call_target="tpu_custom_call" | custom-call | flops 469762048 | bytes 14680064 | tf_op jit(solution)/shard_map/pallas_call | solution.py:280
  28.3 0.6 %copy.14 = f32[128,8]{0,1:T(8,128)} copy(f32[128,8]{0,1:T(8,128)S(1)} %bitcast.12) | data formatting | bytes 8192
  28.9 0.6 %copy.15 = bf16[1,64,512]{2,1,0:T(8,128)(2,1)} copy(bf16[1,64,512]{2,1,0:T(8,128)(2,1)S(1)} %bitcast.11) | data formatting | bytes 131072
  29.5 1.8 %copy.16 = bf16[1,512,3584]{2,1,0:T(8,128)(2,1)} copy(bf16[1,512,3584]{2,1,0:T(8,128)(2,1)S(1)} %bitcast.10) | data formatting | bytes 7340032
  31.4 1.8 %copy.17 = bf16[1,512,3584]{2,1,0:T(8,128)(2,1)} copy(bf16[1,512,3584]{2,1,0:T(8,128)(2,1)S(1)} %bitcast.9) | data formatting | bytes 7340032

commit v2 on v1

--- a/solution.py
+++ b/solution.py
@@ -14,6 +14,7 @@
 SLAB = 16
 BLOCKS = SLAB // CAP
 LANES = 128
+LATE = 5
 
 beta_second = 0.95
 learn_rate = 0.002
@@ -33,11 +34,21 @@
     return lax.broadcasted_iota(jnp.int32, shape, axis)
 
 
+def adamw(hidden_t, scaled, weight, second):
+    grad = dot(hidden_t, scaled)
+    second_new = beta_second * second.astype(f32) + ((1.0 - beta_second) * grad) * grad
+    y = second_new * (1.0 / correct_second)
+    root = y * lax.rsqrt(y)
+    step = (learn_rate * grad) * pl.reciprocal(root + epsilon, approx=True)
+    weight_new = weight.astype(f32) * (1.0 - learn_rate * decay_rate) - step
+    return weight_new.astype(bf16), second_new.astype(bf16)
+
+
 def kernel(
-    nodes, members, plan,
-    ids_ref, gates_ref, grad_hbm, hidden_hbm, weight_hbm, second_hbm,
-    score_out, hidden_out, weight_out, second_out,
-    grads, hidden, weight, second, hidden_t, send, recv, picks, x, scaled, gate,
+    nodes, members, plan, early,
+    ids_hbm, gates_hbm, grad_hbm, hidden_hbm, weight_hbm, second_hbm,
+    score_out, hidden_out, weight, second, hidden_t, scaled,
+    ids_ref, gates_ref, grads, hidden, send, recv, picks, x, gate,
     unscaled, score_send, score_recv,
     load_sem, send_sem, recv_sem, pass_sem, score_send_sem, score_recv_sem,
 ):
@@ -51,10 +62,13 @@
     loads = [
         pltpu.make_async_copy(source, target, load_sem.at[i])
         for i, (source, target) in enumerate(
-            ((grad_hbm, grads), (hidden_hbm, hidden), (weight_hbm, weight), (second_hbm, second))
+            (
+                (ids_hbm, ids_ref), (gates_hbm, gates_ref), (grad_hbm, grads),
+                (hidden_hbm, hidden), (weight_hbm, weight), (second_hbm, second),
+            )
         )
     ]
-    for load in loads:
+    for load in loads[:3]:
         load.start()
 
     barrier = pltpu.get_barrier_semaphore()
@@ -68,6 +82,8 @@
 
     lax.fori_loop(1, devices, greet, 0)
 
+    loads[0].wait()
+    loads[1].wait()
     ids = ids_ref[...]
     hit = ids % EXPERTS_PER_HOST == 0
     hit_one = jnp.where(hit, 1, 0)
@@ -82,27 +98,33 @@
     matched = jnp.sum(jnp.where(hit, gates_ref[...], 0.0), 0, keepdims=True)
     matched = matched.astype(bf16).astype(f32)
 
-    loads[0].wait()
+    loads[2].wait()
+    for load in loads[3:]:
+        load.start()
     place = iota((nodes * SLAB, tokens), 0)
 
     def pack(q):
-        total = jnp.zeros((nodes * SLAB, WIDTH), f32)
-        for c, block in enumerate(plan[q]):
-            mask = place == key + CAP * c
-            if block is None:
-                total += dot(
-                    jnp.where(mask, matched, 0.0).astype(bf16), jnp.ones((tokens, WIDTH), bf16)
-                )
-            else:
-                total += dot(
-                    jnp.where(mask, 1.0, 0.0).astype(bf16),
-                    grads[:, block * WIDTH:(block + 1) * WIDTH],
-                )
+        total = None
+        for c in range(0, len(plan[q]), 2):
+            masks, rights = [], []
+            for block in plan[q][c:c + 2]:
+                mask = place == key + CAP * (c + len(masks))
+                if block is None:
+                    masks.append(jnp.where(mask, matched, 0.0).astype(bf16))
+                    rights.append(jnp.ones((tokens, WIDTH), bf16))
+                else:
+                    masks.append(jnp.where(mask, 1.0, 0.0).astype(bf16))
+                    rights.append(grads[:, block * WIDTH:(block + 1) * WIDTH])
+            part = dot(jnp.concatenate(masks, 1), jnp.concatenate(rights, 0))
+            total = part if total is None else total + part
         send[q] = total.astype(bf16).reshape(nodes, SLAB, WIDTH)
 
+    def turn(i):
+        return nodes // 2 + ((i + 1) // 2) * (1 - 2 * lax.rem(i, 2))
+
     def push(q):
-        def one(k, carry):
-            other = lax.rem(n + k, nodes)
+        def one(i, carry):
+            other = lax.rem(n + turn(i), nodes)
             pltpu.make_async_remote_copy(
                 src_ref=send.at[q, other], dst_ref=recv.at[q, me],
                 send_sem=send_sem.at[q], recv_sem=recv_sem.at[q, me],
@@ -110,7 +132,7 @@
             ).start()
             return carry
 
-        lax.fori_loop(1, nodes, one, 0)
+        lax.fori_loop(0, nodes - 1, one, 0)
         recv[q, me] = send[q, n]
 
     def hand_on(q, source):
@@ -126,18 +148,21 @@
             recv.at[q, source], recv.at[q, source], recv_sem.at[q, source]
         )
 
-    def gather(q):
-        def direct(k, carry):
-            source = l * nodes + lax.rem(n + nodes - k, nodes)
-            arrival(q, source).wait()
-            hand_on(q, source)
+    def relay(q, i):
+        source = l * nodes + lax.rem(n + nodes - turn(i), nodes)
+        arrival(q, source).wait()
+        hand_on(q, source)
+
+    def relay_rest(q, first):
+        def direct(i, carry):
+            relay(q, i)
             return carry
 
-        lax.fori_loop(1, nodes, direct, 0)
-
+        lax.fori_loop(first, nodes - 1, direct, 0)
+
+    def collect(q):
         def passed(k, carry):
-            source = lax.rem(l * nodes + nodes + k, devices)
-            arrival(q, source).wait()
+            arrival(q, lax.rem(l * nodes + nodes + k, devices)).wait()
             return carry
 
         lax.fori_loop(0, devices - nodes, passed, 0)
@@ -167,28 +192,26 @@
         part = dot(x[:, first:last], weight[:, first:last], ((1,), (1,)))
         unscaled[...] = part if q == 0 else unscaled[...] + part
 
-    tall = min(256, units)
-
-    def update(q):
-        first, last = span(q)
+    def update(first, last, relayed=None):
+        tiles = (last - first) // WIDTH
+        share = 0 if relayed is None else -(-(nodes - 1) // tiles)
+        if share > 2:
+            share = 2
 
         def tile(i, carry):
-            rows = pl.ds(pl.multiple_of(lax.rem(i, units // tall) * tall, tall), tall)
-            columns = pl.ds(pl.multiple_of(first + (i // (units // tall)) * WIDTH, WIDTH), WIDTH)
-            grad = dot(hidden_t[rows, :], scaled[:, columns])
-            second_new = (
-                beta_second * second[rows, columns].astype(f32)
-                + ((1.0 - beta_second) * grad) * grad
+            columns = pl.ds(pl.multiple_of(first + i * WIDTH, WIDTH), WIDTH)
+            weight[:, columns], second[:, columns] = adamw(
+                hidden_t[...], scaled[:, columns], weight[:, columns], second[:, columns]
             )
-            y = second_new * (1.0 / correct_second)
-            root = y * lax.rsqrt(y)
-            step = (learn_rate * grad) * pl.reciprocal(root + epsilon, approx=True)
-            weight_new = weight[rows, columns].astype(f32) * (1.0 - learn_rate * decay_rate) - step
-            second_out[rows, columns] = second_new.astype(bf16)
-            weight_out[rows, columns] = weight_new.astype(bf16)
+            for j in range(share):
+                @pl.when(i * share + j < nodes - 1)
+                def _():
+                    relay(relayed, i * share + j)
             return carry
 
-        lax.fori_loop(0, (units // tall) * ((last - first) // WIDTH), tile, 0)
+        lax.fori_loop(0, tiles, tile, 0)
+        if relayed is not None:
+            relay_rest(relayed, min(share * tiles, nodes - 1))
 
     pack(0)
     pl.semaphore_wait(barrier, devices - 1)
@@ -205,17 +228,18 @@
         picks[c * group * CAP:(c + 1) * group * CAP, :] = jnp.where(
             picked_col == wanted + CAP * c, 1.0, 0.0
         ).astype(bf16)
-    loads[1].wait()
+    loads[3].wait()
     hidden_t[...] = hidden[...].astype(f32).T.astype(bf16)
-    loads[2].wait()
-    loads[3].wait()
-
+    loads[4].wait()
+    loads[5].wait()
+
+    relay_rest(0, 0)
     for q in range(len(plan)):
-        gather(q)
+        collect(q)
         unpack(q)
         multiply(q)
         if q < len(plan) - 1:
-            update(q)
+            update(*span(q), relayed=q + 1)
 
     raw = unscaled[...]
     for j in range(0, units, LANES):
@@ -242,7 +266,7 @@
     lax.fori_loop(1, devices, answer, 0)
     score_recv[me] = score_send[(CAP * me) // LANES]
 
-    update(len(plan) - 1)
+    update(span(len(plan) - 1)[0], early)
 
     others = score_recv.at[pl.ds(0, devices - 1)]
     pltpu.make_async_copy(others, others, score_recv_sem).wait()
@@ -267,42 +291,79 @@
                 pltpu.make_async_copy(given, given, pass_sem.at[q]).wait()
 
 
+def finish(
+    early, scores, hidden_grad, weight, second, hidden_t, scaled,
+    score_out, hidden_out, weight_out, second_out,
+    weight_late, second_late, copy_sem,
+):
+    units, features = weight.shape
+    copies = [
+        pltpu.make_async_copy(scores, score_out, copy_sem.at[0]),
+        pltpu.make_async_copy(hidden_grad, hidden_out, copy_sem.at[1]),
+    ]
+    pieces = 4
+    for i in range(pieces):
+        rows = pl.ds(i * (units // pieces), units // pieces)
+        for j, (source, target) in enumerate(((weight, weight_out), (second, second_out))):
+            copies.append(pltpu.make_async_copy(
+                source.at[rows, pl.ds(0, early)], target.at[rows, pl.ds(0, early)],
+                copy_sem.at[2 + 2 * i + j],
+            ))
+    for copy in copies:
+        copy.start()
+    base = 2 + 2 * pieces
+    for i, first in enumerate(range(early, features, WIDTH)):
+        columns, late = pl.ds(first, WIDTH), pl.ds(first - early, WIDTH)
+        weight_late[:, late], second_late[:, late] = adamw(
+            hidden_t[...], scaled[:, columns], weight[:, columns], second[:, columns]
+        )
+        for j, (source, target) in enumerate(((weight_late, weight_out), (second_late, second_out))):
+            copies.append(pltpu.make_async_copy(
+                source.at[:, late], target.at[:, columns], copy_sem.at[base + 2 * i + j]
+            ))
+            copies[-1].start()
+    for copy in copies:
+        copy.wait()
+
+
 def on_device(nodes, members, grad_out, expert_ids, gate_weights, saved_hidden, down_weight, second_moment):
     tokens, features = grad_out.shape
     _, slots, units = saved_hidden.shape
+    chosen = expert_ids.shape[1]
     devices = nodes * members
     group = min(32, devices)
     blocks = [None] + list(range(features // WIDTH))
     plan = [blocks[i:i + BLOCKS] for i in range(0, len(blocks), BLOCKS)]
     chunks = len(plan)
+    early = features - LATE * WIDTH
     small = pl.BlockSpec(memory_space=pltpu.VMEM)
     large = pl.BlockSpec(memory_space=pl.ANY)
-    scores, hidden_grad, new_weight, new_second = pl.pallas_call(
-        functools.partial(kernel, nodes, members, plan),
+    kept = pl.pallas_call(
+        functools.partial(kernel, nodes, members, plan, early),
         out_shape=(
-            pltpu.VMEM((expert_ids.shape[1], tokens), f32),
-            pltpu.VMEM((slots, units), bf16),
-            pltpu.VMEM((units, features), bf16),
-            pltpu.VMEM((units, features), bf16),
-        ),
-        in_specs=[small, small, large, large, large, large],
-        out_specs=(small, small, small, small),
-        scratch_shapes=[
-            pltpu.VMEM((tokens, features), bf16),
+            pltpu.VMEM((chosen, tokens), f32),
             pltpu.VMEM((slots, units), bf16),
             pltpu.VMEM((units, features), bf16),
             pltpu.VMEM((units, features), bf16),
             pltpu.VMEM((units, slots), bf16),
+            pltpu.VMEM((slots, features), bf16),
+        ),
+        in_specs=[large] * 6,
+        out_specs=(small,) * 6,
+        scratch_shapes=[
+            pltpu.VMEM((chosen, tokens), jnp.int32),
+            pltpu.VMEM((chosen, tokens), f32),
+            pltpu.VMEM((tokens, features), bf16),
+            pltpu.VMEM((slots, units), bf16),
             pltpu.VMEM((chunks, nodes, SLAB, WIDTH), bf16),
             pltpu.VMEM((chunks, devices, SLAB, WIDTH), bf16),
             pltpu.VMEM((BLOCKS * group * CAP, group * SLAB), bf16),
-            pltpu.VMEM((slots, features), bf16),
             pltpu.VMEM((slots, features), bf16),
             pltpu.VMEM((slots, WIDTH), f32),
             pltpu.VMEM((slots, units), f32),
             pltpu.VMEM((-(-slots // LANES), 1, LANES), f32),
             pltpu.VMEM((devices, 1, LANES), f32),
-            pltpu.SemaphoreType.DMA((4,)),
+            pltpu.SemaphoreType.DMA((6,)),
             pltpu.SemaphoreType.DMA((chunks,)),
             pltpu.SemaphoreType.DMA((chunks, devices)),
             pltpu.SemaphoreType.DMA((chunks,)),
@@ -313,9 +374,30 @@
             collective_id=0, has_side_effects=True, vmem_limit_bytes=48 * 1024 * 1024
         ),
         cost_estimate=pl.CostEstimate(
-            flops=4 * slots * units * features, bytes_accessed=8 * units * features, transcendentals=0
+            flops=4 * slots * units * features, bytes_accessed=4 * units * features, transcendentals=0
         ),
     )(expert_ids.T, gate_weights.T, grad_out, saved_hidden[0], down_weight[0], second_moment[0])
+    kept = [pltpu.with_memory_space_constraint(a, pltpu.VMEM) for a in kept]
+    scores, hidden_grad, new_weight, new_second = pl.pallas_call(
+        functools.partial(finish, early),
+        out_shape=(
+            jax.ShapeDtypeStruct((chosen, tokens), f32),
+            jax.ShapeDtypeStruct((slots, units), bf16),
+            jax.ShapeDtypeStruct((units, features), bf16),
+            jax.ShapeDtypeStruct((units, features), bf16),
+        ),
+        in_specs=[small] * 6,
+        out_specs=(large,) * 4,
+        scratch_shapes=[
+            pltpu.VMEM((units, features - early), bf16),
+            pltpu.VMEM((units, features - early), bf16),
+            pltpu.SemaphoreType.DMA((10 + 2 * LATE,)),
+        ],
+        compiler_params=pltpu.CompilerParams(vmem_limit_bytes=24 * 1024 * 1024),
+        cost_estimate=pl.CostEstimate(
+            flops=2 * slots * units * LATE * WIDTH, bytes_accessed=4 * units * features, transcendentals=0
+        ),
+    )(*kept)
     return scores.T, hidden_grad[None], new_weight[None], new_second[None]
 
 

time: 33.4 us -> 30.4 us (0.910)
  local copies, waits for them, and re-layouts: 4.9 us -> 0 us
  Pallas kernels: 27.7 us -> 29.6 us
    unnamed x4 -> x0, local copies, waits for them, and re-layouts: 4.9 us -> none
    pallas_call x1 -> x2, Pallas kernels: 27.7 us -> 29.6 us  [the longest x1 26.4 us: on_device(): pl.pallas_call(functools.partial(kernel, nodes, members, plan, early), ou...]
where the time goes in v2:
time: 30.4 us; the launch traced here: 30.2 us
  Pallas kernels  29.6 us (97%)
  between operations  0.64 us (2%)
    pallas_call x1, Pallas kernels, on_device(): pl.pallas_call(functools.partial(kernel, nodes, members, plan, early), ou...  26.4 us
    pallas_call x1, Pallas kernels, on_device(): pl.pallas_call(functools.partial(finish, early), out_shape=(jax.ShapeDtyp...  3.15 us

profile of v2, /device:TPU:0, one launch (start us, length us, event | category | flops | bytes accessed | tf_op | source)
XLA Modules:
  0.0 30.2 jit_solution(5575979464067473323)
XLA Ops:
  0.6 26.4 %shard_map.93 = (f32[8,128]{1,0:T(8,128)S(1)}, bf16[64,512]{1,0:T(8,128)(2,1)S(1)}, bf16[512,3584]{1,0:T(8,128)(2,1)S(1)}, bf16[512,3584]{1,0:T(8,128)(2,1)S(1)}...) custom-call(s32[8,128]{1,0:T(8,128)} %bitcast.12, f32[8,128]{1,0:T(8,128)} %bitcast.13, ...), custom_call_target="tpu_custom_call" | custom-call | flops 469762048 | bytes 7340032 | tf_op jit(solution)/shard_map/pallas_call | solution.py:341
  27.1 3.1 %shard_map.94 = (f32[8,128]{1,0:T(8,128)}, bf16[64,512]{1,0:T(8,128)(2,1)}, bf16[512,3584]{1,0:T(8,128)(2,1)}, bf16[512,3584]{1,0:T(8,128)(2,1)}) custom-call(f32[8,128]{1,0:T(8,128)S(1)} %get-tuple-element.14.scores, bf16[64,512]{1,0:T(8,128)(2,1)S(1)} %get-tuple-element.15.hidden_grad, bf16[512,3584]{1,0:T(8,128)(2,1)S(1)} %get-tuple-element.16.weight, ...), custom_call_target="tpu_custom_call" | custom-call | flops 83886080 | bytes 7340032 | tf_op jit(solution)/shard_map/pallas_call | solution.py:381

commit v3 on v2

--- a/solution.py
+++ b/solution.py
@@ -14,7 +14,7 @@
 SLAB = 16
 BLOCKS = SLAB // CAP
 LANES = 128
-LATE = 5
+LATE = 6
 
 beta_second = 0.95
 learn_rate = 0.002
@@ -36,21 +36,20 @@
 
 def adamw(hidden_t, scaled, weight, second):
     grad = dot(hidden_t, scaled)
-    second_new = beta_second * second.astype(f32) + ((1.0 - beta_second) * grad) * grad
-    y = second_new * (1.0 / correct_second)
-    root = y * lax.rsqrt(y)
-    step = (learn_rate * grad) * pl.reciprocal(root + epsilon, approx=True)
-    weight_new = weight.astype(f32) * (1.0 - learn_rate * decay_rate) - step
-    return weight_new.astype(bf16), second_new.astype(bf16)
+    second_new = second + ((1.0 - beta_second) * grad) * grad
+    root = second_new * lax.rsqrt(second_new) + epsilon * correct_second ** 0.5
+    step = (learn_rate * correct_second ** 0.5 * grad) * pl.reciprocal(root, approx=True)
+    return (weight - step).astype(bf16), second_new.astype(bf16)
 
 
 def kernel(
     nodes, members, plan, early,
     ids_hbm, gates_hbm, grad_hbm, hidden_hbm, weight_hbm, second_hbm,
-    score_out, hidden_out, weight, second, hidden_t, scaled,
-    ids_ref, gates_ref, grads, hidden, send, recv, picks, x, gate,
-    unscaled, score_send, score_recv,
-    load_sem, send_sem, recv_sem, pass_sem, score_send_sem, score_recv_sem,
+    score_out, hidden_out, weight_out, second_out, weight_decayed, second_decayed, hidden_t, scaled,
+    ids_ref, gates_ref, grads, hidden, weight, second, send, recv, picks, x, gate,
+    unscaled, score_send, score_parts, score_recv,
+    load_sem, send_sem, recv_sem, pass_send_sem, pass_recv_sem,
+    part_send_sem, part_recv_sem, score_send_sem, score_recv_sem,
 ):
     n, l = lax.axis_index("node"), lax.axis_index("local")
     devices = nodes * members
@@ -74,13 +73,15 @@
     barrier = pltpu.get_barrier_semaphore()
 
     def greet(k, carry):
-        other = lax.rem(me + k, devices)
         pl.semaphore_signal(
-            barrier, inc=1, device_id=(lax.rem(other, nodes), other // nodes), device_id_type=MESH
+            barrier, inc=1, device_id=(lax.rem(n + k, nodes), l), device_id_type=MESH
         )
         return carry
 
-    lax.fori_loop(1, devices, greet, 0)
+    lax.fori_loop(1, nodes, greet, 0)
+    siblings = [(n, lax.rem(l + k, members)) for k in range(1, members)]
+    for sibling in siblings:
+        pl.semaphore_signal(barrier, inc=1, device_id=sibling, device_id_type=MESH)
 
     loads[0].wait()
     loads[1].wait()
@@ -127,7 +128,7 @@
             other = lax.rem(n + turn(i), nodes)
             pltpu.make_async_remote_copy(
                 src_ref=send.at[q, other], dst_ref=recv.at[q, me],
-                send_sem=send_sem.at[q], recv_sem=recv_sem.at[q, me],
+                send_sem=send_sem.at[q], recv_sem=recv_sem.at[q],
                 device_id=(other, l), device_id_type=MESH,
             ).start()
             return carry
@@ -135,37 +136,21 @@
         lax.fori_loop(0, nodes - 1, one, 0)
         recv[q, me] = send[q, n]
 
-    def hand_on(q, source):
-        for k in range(1, members):
+    def settle(ref, sem):
+        pltpu.make_async_copy(ref, ref, sem).wait()
+
+    def relay(q):
+        settle(recv.at[q, pl.ds(0, nodes - 1)], recv_sem.at[q])
+        mine = recv.at[q, pl.ds(l * nodes, nodes)]
+        for sibling in siblings:
             pltpu.make_async_remote_copy(
-                src_ref=recv.at[q, source], dst_ref=recv.at[q, source],
-                send_sem=pass_sem.at[q], recv_sem=recv_sem.at[q, source],
-                device_id=(n, lax.rem(l + k, members)), device_id_type=MESH,
+                src_ref=mine, dst_ref=mine,
+                send_sem=pass_send_sem.at[q], recv_sem=pass_recv_sem.at[q],
+                device_id=sibling, device_id_type=MESH,
             ).start()
 
-    def arrival(q, source):
-        return pltpu.make_async_copy(
-            recv.at[q, source], recv.at[q, source], recv_sem.at[q, source]
-        )
-
-    def relay(q, i):
-        source = l * nodes + lax.rem(n + nodes - turn(i), nodes)
-        arrival(q, source).wait()
-        hand_on(q, source)
-
-    def relay_rest(q, first):
-        def direct(i, carry):
-            relay(q, i)
-            return carry
-
-        lax.fori_loop(first, nodes - 1, direct, 0)
-
     def collect(q):
-        def passed(k, carry):
-            arrival(q, lax.rem(l * nodes + nodes + k, devices)).wait()
-            return carry
-
-        lax.fori_loop(0, devices - nodes, passed, 0)
+        settle(recv.at[q, pl.ds(0, devices - nodes)], pass_recv_sem.at[q])
 
     def unpack(q):
         for g in range(devices // group):
@@ -192,36 +177,31 @@
         part = dot(x[:, first:last], weight[:, first:last], ((1,), (1,)))
         unscaled[...] = part if q == 0 else unscaled[...] + part
 
-    def update(first, last, relayed=None):
-        tiles = (last - first) // WIDTH
-        share = 0 if relayed is None else -(-(nodes - 1) // tiles)
-        if share > 2:
-            share = 2
-
+    def decay():
         def tile(i, carry):
-            columns = pl.ds(pl.multiple_of(first + i * WIDTH, WIDTH), WIDTH)
-            weight[:, columns], second[:, columns] = adamw(
-                hidden_t[...], scaled[:, columns], weight[:, columns], second[:, columns]
+            columns = pl.ds(pl.multiple_of(i * WIDTH, WIDTH), WIDTH)
+            weight_decayed[:, columns] = weight[:, columns].astype(f32) * (1.0 - learn_rate * decay_rate)
+            second_decayed[:, columns] = second[:, columns].astype(f32) * beta_second
+            return carry
+
+        lax.fori_loop(0, weight.shape[1] // WIDTH, tile, 0)
+
+    def update(first, last):
+        def tile(i, carry):
+            columns = pl.ds(pl.multiple_of(i * WIDTH, WIDTH), WIDTH)
+            weight_out[:, columns], second_out[:, columns] = adamw(
+                hidden_t[...], scaled[:, columns], weight_decayed[:, columns], second_decayed[:, columns]
             )
-            for j in range(share):
-                @pl.when(i * share + j < nodes - 1)
-                def _():
-                    relay(relayed, i * share + j)
             return carry
 
-        lax.fori_loop(0, tiles, tile, 0)
-        if relayed is not None:
-            relay_rest(relayed, min(share * tiles, nodes - 1))
+        lax.fori_loop(first, last, tile, 0)
 
     pack(0)
-    pl.semaphore_wait(barrier, devices - 1)
+    pl.semaphore_wait(barrier, nodes - 1 + members - 1)
     push(0)
     for q in range(1, len(plan)):
         pack(q)
         push(q)
-    for q in range(len(plan)):
-        hand_on(q, me)
-
     picked_row, picked_col = iota((group * CAP, group * SLAB), 0), iota((group * CAP, group * SLAB), 1)
     wanted = (picked_row // CAP) * SLAB + picked_row % CAP
     for c in range(BLOCKS):
@@ -233,13 +213,16 @@
     loads[4].wait()
     loads[5].wait()
 
-    relay_rest(0, 0)
+    decay()
+
+    relay(0)
     for q in range(len(plan)):
         collect(q)
         unpack(q)
         multiply(q)
         if q < len(plan) - 1:
-            update(*span(q), relayed=q + 1)
+            relay(q + 1)
+            update(early[q], early[q + 1])
 
     raw = unscaled[...]
     for j in range(0, units, LANES):
@@ -254,25 +237,35 @@
             part = jnp.concatenate([part, jnp.zeros((LANES - part.shape[0], LANES), f32)], 0)
         score_send[s // LANES] = jnp.sum(part.T, 0, keepdims=True)
 
+    score_parts[l] = jnp.zeros_like(score_send)
+    for sibling in siblings:
+        pltpu.make_async_remote_copy(
+            src_ref=score_send, dst_ref=score_parts.at[l],
+            send_sem=part_send_sem, recv_sem=part_recv_sem,
+            device_id=sibling, device_id_type=MESH,
+        ).start()
+    update(early[-3], early[-2])
+    settle(score_parts.at[pl.ds(0, members - 1)], part_recv_sem)
+    settle(score_parts.at[pl.ds(0, members - 1)], part_send_sem)
+    for k in range(members):
+        score_send[...] += score_parts[k]
+
     def answer(k, carry):
-        other = lax.rem(me + k, devices)
+        other = lax.rem(n + k, nodes)
         pltpu.make_async_remote_copy(
-            src_ref=score_send.at[(CAP * other) // LANES], dst_ref=score_recv.at[me],
+            src_ref=score_send.at[(CAP * (l * nodes + other)) // LANES], dst_ref=score_recv.at[n],
             send_sem=score_send_sem, recv_sem=score_recv_sem,
-            device_id=(lax.rem(other, nodes), other // nodes), device_id_type=MESH,
+            device_id=(other, l), device_id_type=MESH,
         ).start()
         return carry
 
-    lax.fori_loop(1, devices, answer, 0)
-    score_recv[me] = score_send[(CAP * me) // LANES]
-
-    update(span(len(plan) - 1)[0], early)
-
-    others = score_recv.at[pl.ds(0, devices - 1)]
-    pltpu.make_async_copy(others, others, score_recv_sem).wait()
-    sums = score_recv[0:nodes].reshape(nodes, LANES)
-    for k in range(1, members):
-        sums += score_recv[k * nodes:(k + 1) * nodes].reshape(nodes, LANES)
+    lax.fori_loop(1, nodes, answer, 0)
+    score_recv[n] = score_send[(CAP * me) // LANES]
+    update(early[-2], early[-1])
+
+    others = score_recv.at[pl.ds(0, nodes - 1)]
+    settle(others, score_recv_sem)
+    sums = score_recv[...].reshape(nodes, LANES)
     lane = iota((nodes, LANES), 1) - lax.rem(CAP * me, LANES)
     token_score = jnp.zeros((1, tokens), f32)
     for r in range(CAP):
@@ -281,18 +274,14 @@
         token_score += jnp.where(rank == r, column, 0.0)
     score_out[...] = jnp.where(hit, token_score, 0.0)
 
-    pltpu.make_async_copy(others, others, score_send_sem).wait()
+    settle(others, score_send_sem)
     for q in range(len(plan)):
-        sent = send.at[q, pl.ds(0, nodes - 1)]
-        pltpu.make_async_copy(sent, sent, send_sem.at[q]).wait()
-        if members > 1:
-            for _ in range(1):
-                given = recv.at[q, pl.ds(0, nodes * (members - 1))]
-                pltpu.make_async_copy(given, given, pass_sem.at[q]).wait()
+        settle(send.at[q, pl.ds(0, nodes - 1)], send_sem.at[q])
+        settle(recv.at[q, pl.ds(0, devices - nodes)], pass_send_sem.at[q])
 
 
 def finish(
-    early, scores, hidden_grad, weight, second, hidden_t, scaled,
+    early, scores, hidden_grad, weight, second, weight_decayed, second_decayed, hidden_t, scaled,
     score_out, hidden_out, weight_out, second_out,
     weight_late, second_late, copy_sem,
 ):
@@ -315,7 +304,7 @@
     for i, first in enumerate(range(early, features, WIDTH)):
         columns, late = pl.ds(first, WIDTH), pl.ds(first - early, WIDTH)
         weight_late[:, late], second_late[:, late] = adamw(
-            hidden_t[...], scaled[:, columns], weight[:, columns], second[:, columns]
+            hidden_t[...], scaled[:, columns], weight_decayed[:, columns], second_decayed[:, columns]
         )
         for j, (source, target) in enumerate(((weight_late, weight_out), (second_late, second_out))):
             copies.append(pltpu.make_async_copy(
@@ -335,26 +324,32 @@
     blocks = [None] + list(range(features // WIDTH))
     plan = [blocks[i:i + BLOCKS] for i in range(0, len(blocks), BLOCKS)]
     chunks = len(plan)
-    early = features - LATE * WIDTH
+    ahead = features // WIDTH - LATE
+    gaps = [0, (3 * ahead) // 8, (5 * ahead) // 8, ahead]
+    early = ahead * WIDTH
     small = pl.BlockSpec(memory_space=pltpu.VMEM)
     large = pl.BlockSpec(memory_space=pl.ANY)
     kept = pl.pallas_call(
-        functools.partial(kernel, nodes, members, plan, early),
+        functools.partial(kernel, nodes, members, plan, gaps),
         out_shape=(
             pltpu.VMEM((chosen, tokens), f32),
             pltpu.VMEM((slots, units), bf16),
             pltpu.VMEM((units, features), bf16),
             pltpu.VMEM((units, features), bf16),
+            pltpu.VMEM((units, features), f32),
+            pltpu.VMEM((units, features), f32),
             pltpu.VMEM((units, slots), bf16),
             pltpu.VMEM((slots, features), bf16),
         ),
         in_specs=[large] * 6,
-        out_specs=(small,) * 6,
+        out_specs=(small,) * 8,
         scratch_shapes=[
             pltpu.VMEM((chosen, tokens), jnp.int32),
             pltpu.VMEM((chosen, tokens), f32),
             pltpu.VMEM((tokens, features), bf16),
             pltpu.VMEM((slots, units), bf16),
+            pltpu.VMEM((units, features), bf16),
+            pltpu.VMEM((units, features), bf16),
             pltpu.VMEM((chunks, nodes, SLAB, WIDTH), bf16),
             pltpu.VMEM((chunks, devices, SLAB, WIDTH), bf16),
             pltpu.VMEM((BLOCKS * group * CAP, group * SLAB), bf16),
@@ -362,16 +357,20 @@
             pltpu.VMEM((slots, WIDTH), f32),
             pltpu.VMEM((slots, units), f32),
             pltpu.VMEM((-(-slots // LANES), 1, LANES), f32),
-            pltpu.VMEM((devices, 1, LANES), f32),
+            pltpu.VMEM((members, -(-slots // LANES), 1, LANES), f32),
+            pltpu.VMEM((nodes, 1, LANES), f32),
             pltpu.SemaphoreType.DMA((6,)),
             pltpu.SemaphoreType.DMA((chunks,)),
-            pltpu.SemaphoreType.DMA((chunks, devices)),
             pltpu.SemaphoreType.DMA((chunks,)),
+            pltpu.SemaphoreType.DMA((chunks,)),
+            pltpu.SemaphoreType.DMA((chunks,)),
+            pltpu.SemaphoreType.DMA,
+            pltpu.SemaphoreType.DMA,
             pltpu.SemaphoreType.DMA,
             pltpu.SemaphoreType.DMA,
         ],
         compiler_params=pltpu.CompilerParams(
-            collective_id=0, has_side_effects=True, vmem_limit_bytes=48 * 1024 * 1024
+            collective_id=0, has_side_effects=True, vmem_limit_bytes=36 * 1024 * 1024
         ),
         cost_estimate=pl.CostEstimate(
             flops=4 * slots * units * features, bytes_accessed=4 * units * features, transcendentals=0
@@ -386,14 +385,14 @@
             jax.ShapeDtypeStruct((units, features), bf16),
             jax.ShapeDtypeStruct((units, features), bf16),
         ),
-        in_specs=[small] * 6,
+        in_specs=[small] * 8,
         out_specs=(large,) * 4,
         scratch_shapes=[
             pltpu.VMEM((units, features - early), bf16),
             pltpu.VMEM((units, features - early), bf16),
             pltpu.SemaphoreType.DMA((10 + 2 * LATE,)),
         ],
-        compiler_params=pltpu.CompilerParams(vmem_limit_bytes=24 * 1024 * 1024),
+        compiler_params=pltpu.CompilerParams(vmem_limit_bytes=16 * 1024 * 1024),
         cost_estimate=pl.CostEstimate(
             flops=2 * slots * units * LATE * WIDTH, bytes_accessed=4 * units * features, transcendentals=0
         ),

time: 30.4 us -> 26.9 us (0.88)
  Pallas kernels: 29.6 us -> 26.1 us
    pallas_call x1, Pallas kernels: 26.4 us -> 22.9 us  [on_device(): pl.pallas_call(functools.partial(kernel, nodes, members, plan, gaps), out...]
where the time goes in v3:
time: 26.9 us; the launch traced here: 26.7 us
  Pallas kernels  26.1 us (97%)
  between operations  0.64 us (2%)
    pallas_call x1, Pallas kernels, on_device(): pl.pallas_call(functools.partial(kernel, nodes, members, plan, gaps), out...  22.9 us
    pallas_call x1, Pallas kernels, on_device(): pl.pallas_call(functools.partial(finish, early), out_shape=(jax.ShapeDtyp...  3.17 us

profile of v3, /device:TPU:0, one launch (start us, length us, event | category | flops | bytes accessed | tf_op | source)
XLA Modules:
  0.0 26.7 jit_solution(651026051181141486)
XLA Ops:
  0.6 22.9 %shard_map.93 = (f32[8,128]{1,0:T(8,128)S(1)}, bf16[64,512]{1,0:T(8,128)(2,1)S(1)}, bf16[512,3584]{1,0:T(8,128)(2,1)S(1)}, bf16[512,3584]{1,0:T(8,128)(2,1)S(1)}...) custom-call(s32[8,128]{1,0:T(8,128)} %bitcast.12, ...), custom_call_target="tpu_custom_call" | custom-call | flops 469762048 | bytes 7340032 | tf_op jit(solution)/shard_map/pallas_call | solution.py:332
  23.6 3.2 %shard_map.94 = (f32[8,128]{1,0:T(8,128)}, bf16[64,512]{1,0:T(8,128)(2,1)}, bf16[512,3584]{1,0:T(8,128)(2,1)}, bf16[512,3584]{1,0:T(8,128)(2,1)}) custom-call(f32[8,128]{1,0:T(8,128)S(1)} %get-tuple-element.16.scores, bf16[64,512]{1,0:T(8,128)(2,1)S(1)} %get-tuple-element.17.hidden_grad, bf16[512,3584]{1,0:T(8,128)(2,1)S(1)} %get-tuple-element.18.weight, ...), custom_call_target="tpu_custom_call" | custom-call | flops 100663296 | bytes 7340032 | tf_op jit(solution)/shard_map/pallas_call | solution.py:380

commit v4 on v3

--- a/solution.py
+++ b/solution.py
@@ -14,7 +14,7 @@
 SLAB = 16
 BLOCKS = SLAB // CAP
 LANES = 128
-LATE = 6
+LATE = 7
 
 beta_second = 0.95
 learn_rate = 0.002
@@ -47,16 +47,17 @@
     ids_hbm, gates_hbm, grad_hbm, hidden_hbm, weight_hbm, second_hbm,
     score_out, hidden_out, weight_out, second_out, weight_decayed, second_decayed, hidden_t, scaled,
     ids_ref, gates_ref, grads, hidden, weight, second, send, recv, picks, x, gate,
-    unscaled, score_send, score_parts, score_recv,
+    unscaled, back, back_parts, score_sums, score_send, score_recv,
     load_sem, send_sem, recv_sem, pass_send_sem, pass_recv_sem,
-    part_send_sem, part_recv_sem, score_send_sem, score_recv_sem,
+    back_send_sem, back_recv_sem, score_send_sem, score_recv_sem,
 ):
     n, l = lax.axis_index("node"), lax.axis_index("local")
     devices = nodes * members
     me = l * nodes + n
     tokens = grads.shape[0]
     slots, units = hidden.shape
-    group = min(32, devices)
+    group = min(16, nodes)
+    half = nodes * CAP
 
     loads = [
         pltpu.make_async_copy(source, target, load_sem.at[i])
@@ -152,21 +153,35 @@
     def collect(q):
         settle(recv.at[q, pl.ds(0, devices - nodes)], pass_recv_sem.at[q])
 
-    def unpack(q):
-        for g in range(devices // group):
-            landed = recv[q, g * group:(g + 1) * group].reshape(group * SLAB, WIDTH)
+    def unpack(q, member, scored=False):
+        rows = group * CAP
+        for g in range(nodes // group):
+            source = member * nodes + g * group
+            landed = recv[q, pl.ds(source, group)].reshape(group * SLAB, WIDTH)
             chosen = dot(picks[...], landed)
-            rows = group * CAP
-            here = slice(g * rows, (g + 1) * rows)
+            here = pl.ds(pl.multiple_of(source * CAP, rows), rows)
+            local = slice(g * rows, (g + 1) * rows)
+            if None in plan[q]:
+                c = plan[q].index(None)
+                gate[here, :] = chosen[c * rows:(c + 1) * rows]
+            factor = gate[here, :]
+            sums = None
             for c, block in enumerate(plan[q]):
                 if block is None:
-                    gate[here, :] = chosen[c * rows:(c + 1) * rows]
-            for c, block in enumerate(plan[q]):
-                if block is not None:
-                    part = chosen[c * rows:(c + 1) * rows]
-                    columns = slice(block * WIDTH, (block + 1) * WIDTH)
-                    x[here, columns] = part.astype(bf16)
-                    scaled[here, columns] = (gate[here, :] * part).astype(bf16)
+                    continue
+                part = chosen[c * rows:(c + 1) * rows]
+                columns = slice(block * WIDTH, (block + 1) * WIDTH)
+                x[here, columns] = part.astype(bf16)
+                scaled[here, columns] = (factor * part).astype(bf16)
+                if scored:
+                    against = back[here, columns].astype(f32)
+                    for k in range(members - 1):
+                        against += back_parts[k, local, columns].astype(f32)
+                    term = part * against
+                    sums = term if sums is None else sums + term
+            if scored:
+                sums = sums[:, :LANES] + sums[:, LANES:]
+                score_sums[local, :] = sums if q == 0 else score_sums[local, :] + sums
 
     def span(q):
         blocks = [b for b in plan[q] if b is not None]
@@ -202,71 +217,70 @@
     for q in range(1, len(plan)):
         pack(q)
         push(q)
+    loads[3].wait()
+    loads[4].wait()
+    features = weight.shape[1]
+    stripe = 2 * WIDTH
+    for j in range(0, features, stripe):
+        back[:, j:j + stripe] = dot(hidden[...], weight[:, j:j + stripe]).astype(back.dtype)
+    for k in range(1, members):
+        other = lax.rem(l + k, members)
+        pltpu.make_async_remote_copy(
+            src_ref=back.at[pl.ds(pl.multiple_of(other * half, half), half)], dst_ref=back_parts.at[k - 1],
+            send_sem=back_send_sem.at[k - 1], recv_sem=back_recv_sem.at[k - 1],
+            device_id=(n, other), device_id_type=MESH,
+        ).start()
+
     picked_row, picked_col = iota((group * CAP, group * SLAB), 0), iota((group * CAP, group * SLAB), 1)
     wanted = (picked_row // CAP) * SLAB + picked_row % CAP
     for c in range(BLOCKS):
         picks[c * group * CAP:(c + 1) * group * CAP, :] = jnp.where(
             picked_col == wanted + CAP * c, 1.0, 0.0
         ).astype(bf16)
-    loads[3].wait()
     hidden_t[...] = hidden[...].astype(f32).T.astype(bf16)
-    loads[4].wait()
     loads[5].wait()
 
     decay()
 
-    relay(0)
+    for k in range(members - 1):
+        settle(back_parts.at[k], back_recv_sem.at[k])
     for q in range(len(plan)):
+        relay(q)
+        unpack(q, l, scored=True)
+        if q == len(plan) - 1:
+            for s in range(0, half, LANES):
+                part = score_sums[s:min(s + LANES, half), :]
+                if part.shape[0] < LANES:
+                    part = jnp.concatenate([part, jnp.zeros((LANES - part.shape[0], LANES), f32)], 0)
+                score_send[s // LANES] = jnp.sum(part.T, 0, keepdims=True)
+
+            def answer(i, carry):
+                other = lax.rem(n + turn(i), nodes)
+                pltpu.make_async_remote_copy(
+                    src_ref=score_send.at[(CAP * other) // LANES], dst_ref=score_recv.at[n],
+                    send_sem=score_send_sem, recv_sem=score_recv_sem,
+                    device_id=(other, l), device_id_type=MESH,
+                ).start()
+                return carry
+
+            lax.fori_loop(0, nodes - 1, answer, 0)
+            score_recv[n] = score_send[(CAP * n) // LANES]
         collect(q)
-        unpack(q)
+        for k in range(1, members):
+            unpack(q, lax.rem(l + k, members))
         multiply(q)
         if q < len(plan) - 1:
-            relay(q + 1)
             update(early[q], early[q + 1])
 
     raw = unscaled[...]
     for j in range(0, units, LANES):
         hidden_out[:, j:j + LANES] = (gate[:, :LANES] * raw[:, j:j + LANES]).astype(bf16)
-    terms = raw * hidden[...].astype(f32)
-    folded = terms[:, :LANES]
-    for j in range(LANES, units, LANES):
-        folded += terms[:, j:j + LANES]
-    for s in range(0, slots, LANES):
-        part = folded[s:s + LANES]
-        if part.shape[0] < LANES:
-            part = jnp.concatenate([part, jnp.zeros((LANES - part.shape[0], LANES), f32)], 0)
-        score_send[s // LANES] = jnp.sum(part.T, 0, keepdims=True)
-
-    score_parts[l] = jnp.zeros_like(score_send)
-    for sibling in siblings:
-        pltpu.make_async_remote_copy(
-            src_ref=score_send, dst_ref=score_parts.at[l],
-            send_sem=part_send_sem, recv_sem=part_recv_sem,
-            device_id=sibling, device_id_type=MESH,
-        ).start()
-    update(early[-3], early[-2])
-    settle(score_parts.at[pl.ds(0, members - 1)], part_recv_sem)
-    settle(score_parts.at[pl.ds(0, members - 1)], part_send_sem)
-    for k in range(members):
-        score_send[...] += score_parts[k]
-
-    def answer(k, carry):
-        other = lax.rem(n + k, nodes)
-        pltpu.make_async_remote_copy(
-            src_ref=score_send.at[(CAP * (l * nodes + other)) // LANES], dst_ref=score_recv.at[n],
-            send_sem=score_send_sem, recv_sem=score_recv_sem,
-            device_id=(other, l), device_id_type=MESH,
-        ).start()
-        return carry
-
-    lax.fori_loop(1, nodes, answer, 0)
-    score_recv[n] = score_send[(CAP * me) // LANES]
     update(early[-2], early[-1])
 
     others = score_recv.at[pl.ds(0, nodes - 1)]
     settle(others, score_recv_sem)
     sums = score_recv[...].reshape(nodes, LANES)
-    lane = iota((nodes, LANES), 1) - lax.rem(CAP * me, LANES)
+    lane = iota((nodes, LANES), 1) - lax.rem(CAP * n, LANES)
     token_score = jnp.zeros((1, tokens), f32)
     for r in range(CAP):
         column = jnp.sum(jnp.where(lane == r, sums, 0.0), 1, keepdims=True)
@@ -275,6 +289,8 @@
     score_out[...] = jnp.where(hit, token_score, 0.0)
 
     settle(others, score_send_sem)
+    for k in range(members - 1):
+        settle(back_parts.at[k], back_send_sem.at[k])
     for q in range(len(plan)):
         settle(send.at[q, pl.ds(0, nodes - 1)], send_sem.at[q])
         settle(recv.at[q, pl.ds(0, devices - nodes)], pass_send_sem.at[q])
@@ -320,12 +336,14 @@
     _, slots, units = saved_hidden.shape
     chosen = expert_ids.shape[1]
     devices = nodes * members
-    group = min(32, devices)
+    group = min(16, nodes)
+    half = nodes * CAP
+    back_type = f32 if slots * features <= 1 << 20 else bf16
     blocks = [None] + list(range(features // WIDTH))
     plan = [blocks[i:i + BLOCKS] for i in range(0, len(blocks), BLOCKS)]
     chunks = len(plan)
     ahead = features // WIDTH - LATE
-    gaps = [0, (3 * ahead) // 8, (5 * ahead) // 8, ahead]
+    gaps = [0, (4 * ahead) // 7, ahead]
     early = ahead * WIDTH
     small = pl.BlockSpec(memory_space=pltpu.VMEM)
     large = pl.BlockSpec(memory_space=pl.ANY)
@@ -356,21 +374,23 @@
             pltpu.VMEM((slots, features), bf16),
             pltpu.VMEM((slots, WIDTH), f32),
             pltpu.VMEM((slots, units), f32),
-            pltpu.VMEM((-(-slots // LANES), 1, LANES), f32),
-            pltpu.VMEM((members, -(-slots // LANES), 1, LANES), f32),
+            pltpu.VMEM((slots, features), back_type),
+            pltpu.VMEM((members - 1, half, features), back_type),
+            pltpu.VMEM((half, LANES), f32),
+            pltpu.VMEM((-(-half // LANES), 1, LANES), f32),
             pltpu.VMEM((nodes, 1, LANES), f32),
             pltpu.SemaphoreType.DMA((6,)),
             pltpu.SemaphoreType.DMA((chunks,)),
             pltpu.SemaphoreType.DMA((chunks,)),
             pltpu.SemaphoreType.DMA((chunks,)),
             pltpu.SemaphoreType.DMA((chunks,)),
-            pltpu.SemaphoreType.DMA,
-            pltpu.SemaphoreType.DMA,
+            pltpu.SemaphoreType.DMA((members - 1,)),
+            pltpu.SemaphoreType.DMA((members - 1,)),
             pltpu.SemaphoreType.DMA,
             pltpu.SemaphoreType.DMA,
         ],
         compiler_params=pltpu.CompilerParams(
-            collective_id=0, has_side_effects=True, vmem_limit_bytes=36 * 1024 * 1024
+            collective_id=0, has_side_effects=True, vmem_limit_bytes=40 * 1024 * 1024
         ),
         cost_estimate=pl.CostEstimate(
             flops=4 * slots * units * features, bytes_accessed=4 * units * features, transcendentals=0

time: 26.9 us -> 25.2 us (0.937)
  Pallas kernels: 26.1 us -> 24.4 us
    pallas_call x1, Pallas kernels: 22.9 us -> 21.2 us  [on_device(): pl.pallas_call(functools.partial(kernel, nodes, members, plan, gaps), out...]
where the time goes in v4:
time: 25.2 us; the launch traced here: 25.1 us
  Pallas kernels  24.4 us (97%)
  between operations  0.64 us (3%)
    pallas_call x1, Pallas kernels, on_device(): pl.pallas_call(functools.partial(kernel, nodes, members, plan, gaps), out...  21.2 us
    pallas_call x1, Pallas kernels, on_device(): pl.pallas_call(functools.partial(finish, early), out_shape=(jax.ShapeDtyp...  3.19 us

profile of v4, /device:TPU:0, one launch (start us, length us, event | category | flops | bytes accessed | tf_op | source)
XLA Modules:
  0.0 25.1 jit_solution(2775305465028442075)
XLA Ops:
  0.6 21.2 %shard_map.93 = (f32[8,128]{1,0:T(8,128)S(1)}, bf16[64,512]{1,0:T(8,128)(2,1)S(1)}, bf16[512,3584]{1,0:T(8,128)(2,1)S(1)}, bf16[512,3584]{1,0:T(8,128)(2,1)S(1)}...) custom-call(s32[8,128]{1,0:T(8,128)} %bitcast.12, ...), custom_call_target="tpu_custom_call" | custom-call | flops 469762048 | bytes 7340032 | tf_op jit(solution)/shard_map/pallas_call | solution.py:350
  21.9 3.2 %shard_map.94 = (f32[8,128]{1,0:T(8,128)}, bf16[64,512]{1,0:T(8,128)(2,1)}, bf16[512,3584]{1,0:T(8,128)(2,1)}, bf16[512,3584]{1,0:T(8,128)(2,1)}) custom-call(f32[8,128]{1,0:T(8,128)S(1)} %get-tuple-element.16.scores, bf16[64,512]{1,0:T(8,128)(2,1)S(1)} %get-tuple-element.17.hidden_grad, bf16[512,3584]{1,0:T(8,128)(2,1)S(1)} %get-tuple-element.18.weight, ...), custom_call_target="tpu_custom_call" | custom-call | flops 117440512 | bytes 7340032 | tf_op jit(solution)/shard_map/pallas_call | solution.py:400

commit v5 on v4

--- a/solution.py
+++ b/solution.py
@@ -14,7 +14,7 @@
 SLAB = 16
 BLOCKS = SLAB // CAP
 LANES = 128
-LATE = 7
+LATE = 9
 
 beta_second = 0.95
 learn_rate = 0.002
@@ -79,7 +79,7 @@
         )
         return carry
 
-    lax.fori_loop(1, nodes, greet, 0)
+    lax.fori_loop(1, nodes, greet, 0, unroll=nodes <= 16)
     siblings = [(n, lax.rem(l + k, members)) for k in range(1, members)]
     for sibling in siblings:
         pl.semaphore_signal(barrier, inc=1, device_id=sibling, device_id_type=MESH)
@@ -134,7 +134,7 @@
             ).start()
             return carry
 
-        lax.fori_loop(0, nodes - 1, one, 0)
+        lax.fori_loop(0, nodes - 1, one, 0, unroll=nodes <= 16)
         recv[q, me] = send[q, n]
 
     def settle(ref, sem):
@@ -189,7 +189,7 @@
 
     def multiply(q):
         first, last = span(q)
-        part = dot(x[:, first:last], weight[:, first:last], ((1,), (1,)))
+        part = dot(weight[:, first:last], x[:, first:last], ((1,), (1,)))
         unscaled[...] = part if q == 0 else unscaled[...] + part
 
     def decay():
@@ -263,7 +263,7 @@
                 ).start()
                 return carry
 
-            lax.fori_loop(0, nodes - 1, answer, 0)
+            lax.fori_loop(0, nodes - 1, answer, 0, unroll=nodes <= 16)
             score_recv[n] = score_send[(CAP * n) // LANES]
         collect(q)
         for k in range(1, members):
@@ -272,7 +272,7 @@
         if q < len(plan) - 1:
             update(early[q], early[q + 1])
 
-    raw = unscaled[...]
+    raw = unscaled[...].T
     for j in range(0, units, LANES):
         hidden_out[:, j:j + LANES] = (gate[:, :LANES] * raw[:, j:j + LANES]).astype(bf16)
     update(early[-2], early[-1])
@@ -343,7 +343,7 @@
     plan = [blocks[i:i + BLOCKS] for i in range(0, len(blocks), BLOCKS)]
     chunks = len(plan)
     ahead = features // WIDTH - LATE
-    gaps = [0, (4 * ahead) // 7, ahead]
+    gaps = [0, (4 * ahead) // 5, ahead]
     early = ahead * WIDTH
     small = pl.BlockSpec(memory_space=pltpu.VMEM)
     large = pl.BlockSpec(memory_space=pl.ANY)
@@ -373,7 +373,7 @@
             pltpu.VMEM((BLOCKS * group * CAP, group * SLAB), bf16),
             pltpu.VMEM((slots, features), bf16),
             pltpu.VMEM((slots, WIDTH), f32),
-            pltpu.VMEM((slots, units), f32),
+            pltpu.VMEM((units, slots), f32),
             pltpu.VMEM((slots, features), back_type),
             pltpu.VMEM((members - 1, half, features), back_type),
             pltpu.VMEM((half, LANES), f32),

time: 25.2 us -> 25.1 us (level)
  no operation moved by 1% of the time
where the time goes in v5:
time: 25.1 us; the launch traced here: 24.9 us
  Pallas kernels  24.2 us (96%)
  between operations  0.64 us (3%)
    pallas_call x1, Pallas kernels, on_device(): pl.pallas_call(functools.partial(kernel, nodes, members, plan, gaps), out...  21 us
    pallas_call x1, Pallas kernels, on_device(): pl.pallas_call(functools.partial(finish, early), out_shape=(jax.ShapeDtyp...  3.23 us

profile of v5, /device:TPU:0, one launch (start us, length us, event | category | flops | bytes accessed | tf_op | source)
XLA Modules:
  0.0 24.9 jit_solution(11264613998176635422)
XLA Ops:
  0.6 21.0 %shard_map.93 = (f32[8,128]{1,0:T(8,128)S(1)}, bf16[64,512]{1,0:T(8,128)(2,1)S(1)}, bf16[512,3584]{1,0:T(8,128)(2,1)S(1)}, bf16[512,3584]{1,0:T(8,128)(2,1)S(1)}...) custom-call(s32[8,128]{1,0:T(8,128)} %bitcast.12, ...), custom_call_target="tpu_custom_call" | custom-call | flops 469762048 | bytes 7340032 | tf_op jit(solution)/shard_map/pallas_call | solution.py:350
  21.6 3.2 %shard_map.94 = (f32[8,128]{1,0:T(8,128)}, bf16[64,512]{1,0:T(8,128)(2,1)}, bf16[512,3584]{1,0:T(8,128)(2,1)}, bf16[512,3584]{1,0:T(8,128)(2,1)}) custom-call(f32[8,128]{1,0:T(8,128)S(1)} %get-tuple-element.16.scores, bf16[64,512]{1,0:T(8,128)(2,1)S(1)} %get-tuple-element.17.hidden_grad, bf16[512,3584]{1,0:T(8,128)(2,1)S(1)} %get-tuple-element.18.weight, ...), custom_call_target="tpu_custom_call" | custom-call | flops 150994944 | bytes 7340032 | tf_op jit(solution)/shard_map/pallas_call | solution.py:400

commit v6 on v5

--- a/solution.py
+++ b/solution.py
@@ -14,7 +14,7 @@
 SLAB = 16
 BLOCKS = SLAB // CAP
 LANES = 128
-LATE = 9
+LATE = 2
 
 beta_second = 0.95
 learn_rate = 0.002
@@ -68,9 +68,6 @@
             )
         )
     ]
-    for load in loads[:3]:
-        load.start()
-
     barrier = pltpu.get_barrier_semaphore()
 
     def greet(k, carry):
@@ -84,6 +81,8 @@
     for sibling in siblings:
         pl.semaphore_signal(barrier, inc=1, device_id=sibling, device_id_type=MESH)
 
+    for load in loads[:3]:
+        load.start()
     loads[0].wait()
     loads[1].wait()
     ids = ids_ref[...]
@@ -343,7 +342,7 @@
     plan = [blocks[i:i + BLOCKS] for i in range(0, len(blocks), BLOCKS)]
     chunks = len(plan)
     ahead = features // WIDTH - LATE
-    gaps = [0, (4 * ahead) // 5, ahead]
+    gaps = [0, (5 * ahead) // 12, ahead]
     early = ahead * WIDTH
     small = pl.BlockSpec(memory_space=pltpu.VMEM)
     large = pl.BlockSpec(memory_space=pl.ANY)

time: 25.1 us -> 25.3 us (level)
  Pallas kernels: 24.2 us -> 24.5 us
    pallas_call x1, Pallas kernels: 21 us -> 21.3 us  [on_device(): pl.pallas_call(functools.partial(kernel, nodes, members, plan, gaps), out...]
where the time goes in v6:
time: 25.3 us; the launch traced here: 25.1 us
  Pallas kernels  24.5 us (97%)
  between operations  0.64 us (3%)
    pallas_call x1, Pallas kernels, on_device(): pl.pallas_call(functools.partial(kernel, nodes, members, plan, gaps), out...  21.3 us
    pallas_call x1, Pallas kernels, on_device(): pl.pallas_call(functools.partial(finish, early), out_shape=(jax.ShapeDtyp...  3.12 us

profile of v6, /device:TPU:0, one launch (start us, length us, event | category | flops | bytes accessed | tf_op | source)
XLA Modules:
  0.0 25.1 jit_solution(14920266981136813276)
XLA Ops:
  0.6 21.3 %shard_map.93 = (f32[8,128]{1,0:T(8,128)S(1)}, bf16[64,512]{1,0:T(8,128)(2,1)S(1)}, bf16[512,3584]{1,0:T(8,128)(2,1)S(1)}, bf16[512,3584]{1,0:T(8,128)(2,1)S(1)}...) custom-call(s32[8,128]{1,0:T(8,128)} %bitcast.12, ...), custom_call_target="tpu_custom_call" | custom-call | flops 469762048 | bytes 7340032 | tf_op jit(solution)/shard_map/pallas_call | solution.py:349
  22.0 3.1 %shard_map.94 = (f32[8,128]{1,0:T(8,128)}, bf16[64,512]{1,0:T(8,128)(2,1)}, bf16[512,3584]{1,0:T(8,128)(2,1)}, bf16[512,3584]{1,0:T(8,128)(2,1)}) custom-call(f32[8,128]{1,0:T(8,128)S(1)} %get-tuple-element.16.scores, bf16[64,512]{1,0:T(8,128)(2,1)S(1)} %get-tuple-element.17.hidden_grad, bf16[512,3584]{1,0:T(8,128)(2,1)S(1)} %get-tuple-element.18.weight, ...), custom_call_target="tpu_custom_call" | custom-call | flops 33554432 | bytes 7340032 | tf_op jit(solution)/shard_map/pallas_call | solution.py:399

commit v7 on v6

--- a/solution.py
+++ b/solution.py
@@ -14,7 +14,7 @@
 SLAB = 16
 BLOCKS = SLAB // CAP
 LANES = 128
-LATE = 2
+LATE = 7
 
 beta_second = 0.95
 learn_rate = 0.002
@@ -121,7 +121,7 @@
         send[q] = total.astype(bf16).reshape(nodes, SLAB, WIDTH)
 
     def turn(i):
-        return nodes // 2 + ((i + 1) // 2) * (1 - 2 * lax.rem(i, 2))
+        return 1 + lax.rem((i + 1) * (nodes // 2 - 1), nodes - 1)
 
     def push(q):
         def one(i, carry):
@@ -342,7 +342,7 @@
     plan = [blocks[i:i + BLOCKS] for i in range(0, len(blocks), BLOCKS)]
     chunks = len(plan)
     ahead = features // WIDTH - LATE
-    gaps = [0, (5 * ahead) // 12, ahead]
+    gaps = [0, (4 * ahead) // 7, ahead]
     early = ahead * WIDTH
     small = pl.BlockSpec(memory_space=pltpu.VMEM)
     large = pl.BlockSpec(memory_space=pl.ANY)

time: 25.3 us -> 24.9 us (0.984)
  Pallas kernels: 24.5 us -> 24.1 us
    pallas_call x1, Pallas kernels: 21.3 us -> 20.9 us  [on_device(): pl.pallas_call(functools.partial(kernel, nodes, members, plan, gaps), out...]
where the time goes in v7:
time: 24.9 us; the launch traced here: 24.7 us
  Pallas kernels  24.1 us (97%)
  between operations  0.64 us (3%)
    pallas_call x1, Pallas kernels, on_device(): pl.pallas_call(functools.partial(kernel, nodes, members, plan, gaps), out...  20.9 us
    pallas_call x1, Pallas kernels, on_device(): pl.pallas_call(functools.partial(finish, early), out_shape=(jax.ShapeDtyp...  3.19 us

profile of v7, /device:TPU:0, one launch (start us, length us, event | category | flops | bytes accessed | tf_op | source)
XLA Modules:
  0.0 24.7 jit_solution(545090610362125965)
XLA Ops:
  0.6 20.9 %shard_map.93 = (f32[8,128]{1,0:T(8,128)S(1)}, bf16[64,512]{1,0:T(8,128)(2,1)S(1)}, bf16[512,3584]{1,0:T(8,128)(2,1)S(1)}, bf16[512,3584]{1,0:T(8,128)(2,1)S(1)}...) custom-call(s32[8,128]{1,0:T(8,128)} %bitcast.12, ...), custom_call_target="tpu_custom_call" | custom-call | flops 469762048 | bytes 7340032 | tf_op jit(solution)/shard_map/pallas_call | solution.py:349
  21.6 3.2 %shard_map.94 = (f32[8,128]{1,0:T(8,128)}, bf16[64,512]{1,0:T(8,128)(2,1)}, bf16[512,3584]{1,0:T(8,128)(2,1)}, bf16[512,3584]{1,0:T(8,128)(2,1)}) custom-call(f32[8,128]{1,0:T(8,128)S(1)} %get-tuple-element.16.scores, bf16[64,512]{1,0:T(8,128)(2,1)S(1)} %get-tuple-element.17.hidden_grad, bf16[512,3584]{1,0:T(8,128)(2,1)S(1)} %get-tuple-element.18.weight, ...), custom_call_target="tpu_custom_call" | custom-call | flops 117440512 | bytes 7340032 | tf_op jit(solution)/shard_map/pallas_call | solution.py:399
